TPU v7x, 256 devices: a whole 4x4x8 slice. The times are simulated.
256 devices in a mesh: pool: 8 (over z), tp: 16 (over y_lo, x, core), rep: 2 (over y_hi).
Axes of the slice: x: 4, y: 4 (y_hi: 2, y_lo: 2; y = y_hi * 2 + y_lo), z: 8, core: 2. Of those that a mesh axis runs over, the one named last changes fastest.
Arguments:
- queries: bfloat16 [2, 8, 4, 256, 16384], P('rep', 'pool', None, None, 'tp'), may hold values from -48 to 48
- pool_cache: bfloat16 [512, 8, 128, 256], P('pool', None, 'tp'), may hold values from -6 to 6
- new_kv: bfloat16 [2, 8, 4, 2, 8, 128, 256], P('rep', 'pool', None, None, None, 'tp'), may hold values from -16 to 16
- block_ids: int32 [2, 8, 4, 12], P('rep'), may hold values from 0 to 511, as said below
- prefix_count: int32 [2, 8], P('rep'), may hold values from 6 to 12, as said below
- new_ids: int32 [2, 8, 4, 2], P('rep'), may hold values from 0 to 63, as said below
Outputs:
- attn_out: bfloat16 [2, 8, 4, 256, 16384], P('rep', 'pool', None, None, 'tp')
- stored_new: bfloat16 [2, 64, 8, 128, 256], P('rep', 'pool', None, 'tp')
Inputs may be any that keep to these rules, and one draw needn't show every extreme that they name: `block_ids`: an id names slot id % 64 of holder id // 64. In every list of 12 entries at most 2 entries name one holder, and some holder is named by exactly 2. `prefix_count`: some prompt has all 12 entries live. `new_ids`: within one index of the first dimension every id appears exactly once. The ids of one prompt name each holder id // 8 exactly once.
All inputs are finite; a program needn't handle non-finite values.
Results may differ from a plain program's by a relative error of at most 0.0034.
Values may be sent and summed in bfloat16 or wider, within the bound.
A program may use at most 128 MiB of HBM per device.

v0:
```python
import functools
import math

import jax
import jax.numpy as jnp
from jax import lax
from jax.experimental import pallas as pl
from jax.experimental.pallas import tpu as pltpu
from jax.sharding import PartitionSpec as P

MESH = pl.DeviceIdType.MESH
POOL = 8
CHIPS = 8
CORES = 2
LAYERS = 4
LIST = 12
SLOTS = 64
TOK = 8
CAP = 2
ROWS = CAP * TOK
HEADS = 8
HD = 128
QH = 8
SPAN = 256
ENTRIES = 8
DISTANCE = (4, 3, 5, 2, 6, 1, 7)
FIRST_FAR = 2
SOURCES = FIRST_FAR + len(DISTANCE)
GROUPS = ((0, 2), (2, 3), (3, 5), (5, 7), (7, 9))
N_GROUPS = len(GROUPS)
MASKED = -1e30
TO_LOG2 = math.log2(math.e) / math.sqrt(HD)


def interleave(first, second):
    first = first.astype(jnp.float32)
    second = second.astype(jnp.float32)
    pieces = []
    for head in range(HEADS):
        rows = slice(head * TOK, (head + 1) * TOK)
        pieces += [first[rows], second[rows]]
    return jnp.concatenate(pieces, axis=0).astype(jnp.bfloat16)


def kernel(
    ids, counts, new_ids, q_in, cache_in, new_in, attn_out, stored_out,
    cache, new, q, zsend, zbuf, kv, nsend, nrecv, placed, attn, top, total, acc,
    in_sem, zs, zr, ps, pr, ss, sr, ns, nr, out_sem,
):
    pool = lax.axis_index("pool")
    tp = lax.axis_index("tp")
    core = lax.rem(tp, CORES)
    chip = lax.div(tp, CORES)

    def pool_peer(distance):
        return lax.rem(pool + distance, POOL)

    def chip_peer(step):
        return lax.rem(chip + step, CHIPS)

    sibling = {"tp": chip * CORES + 1 - core}

    loads = [
        pltpu.make_async_copy(cache_in, cache, in_sem.at[0]),
        pltpu.make_async_copy(new_in, new, in_sem.at[1]),
        pltpu.make_async_copy(q_in, q, in_sem.at[2]),
    ]
    for load in loads:
        load.start()

    barrier = pltpu.get_barrier_semaphore()
    for distance in DISTANCE:
        pl.semaphore_signal(barrier, inc=1, device_id={"pool": pool_peer(distance)}, device_id_type=MESH)
    for step in range(1, CHIPS):
        pl.semaphore_signal(
            barrier, inc=1, device_id={"tp": chip_peer(step) * CORES + core}, device_id_type=MESH
        )
    pl.semaphore_signal(barrier, inc=1, device_id=sibling, device_id_type=MESH)

    def prepare(layer):
        for place in range(FIRST_FAR - 1, SOURCES):
            distance = 0 if place < FIRST_FAR else DISTANCE[place - FIRST_FAR]
            prompt = pool_peer(distance)
            live = counts[0, prompt]
            first = jnp.int32(0)
            last = jnp.int32(0)
            found = [
                ((ids[prompt, layer, j] >> 6) == pool) & (j < live) for j in range(LIST)
            ]
            slot = [ids[prompt, layer, j] & (SLOTS - 1) for j in range(LIST)]
            for j in range(LIST):
                last = jnp.where(found[j], slot[j], last)
                first = jnp.where(found[LIST - 1 - j], slot[LIST - 1 - j], first)
            rows = interleave(cache[first], cache[last])
            if place < FIRST_FAR:
                zbuf[layer, place] = rows
            else:
                zsend[layer, place - FIRST_FAR] = rows
        zbuf[layer, 0] = interleave(new[2 * layer], new[2 * layer + 1])

    def z_copy(layer, index):
        return pltpu.make_async_remote_copy(
            src_ref=zsend.at[layer, index],
            dst_ref=zbuf.at[layer, FIRST_FAR + index],
            send_sem=zs.at[layer, index],
            recv_sem=zr.at[layer, index],
            device_id={"pool": pool_peer(DISTANCE[index])},
            device_id_type=MESH,
        )

    def n_copy(index):
        return pltpu.make_async_remote_copy(
            src_ref=nsend.at[index],
            dst_ref=nrecv.at[1 + index],
            send_sem=ns.at[index],
            recv_sem=nr.at[index],
            device_id={"pool": pool_peer(DISTANCE[index])},
            device_id_type=MESH,
        )

    def plane_copy(layer, group, step):
        low, high = GROUPS[group]
        target = chip_peer(step)
        return pltpu.make_async_remote_copy(
            src_ref=zbuf.at[layer, pl.ds(low, high - low), pl.ds(pl.multiple_of(target * ROWS, ROWS), ROWS)],
            dst_ref=kv.at[
                layer,
                pl.ds(low, high - low),
                pl.ds(pl.multiple_of((core * CHIPS + chip) * ROWS, ROWS), ROWS),
            ],
            send_sem=ps.at[layer, group, step - 1],
            recv_sem=pr.at[layer, group, step - 1],
            device_id={"tp": target * CORES + core},
            device_id_type=MESH,
        )

    def sibling_copy(layer, group):
        low, high = GROUPS[group]
        half = (
            layer,
            pl.ds(low, high - low),
            pl.ds(pl.multiple_of(core * CHIPS * ROWS, CHIPS * ROWS), CHIPS * ROWS),
        )
        return pltpu.make_async_remote_copy(
            src_ref=kv.at[half],
            dst_ref=kv.at[half],
            send_sem=ss.at[layer, group],
            recv_sem=sr.at[layer, group],
            device_id=sibling,
            device_id_type=MESH,
        )

    def z_send(layer):
        for index in range(len(DISTANCE)):
            z_copy(layer, index).start()

    def spread(layer, group):
        low, high = GROUPS[group]
        for place in range(max(low, FIRST_FAR), high):
            z_copy(layer, place - FIRST_FAR).wait_recv()
        for step in range(1, CHIPS):
            plane_copy(layer, group, step).start()
        mine = zbuf[layer, pl.ds(low, high - low), pl.ds(pl.multiple_of(chip * ROWS, ROWS), ROWS)]
        kv[
            layer,
            pl.ds(low, high - low),
            pl.ds(pl.multiple_of((core * CHIPS + chip) * ROWS, ROWS), ROWS),
        ] = mine

    def share(layer, group):
        for step in range(1, CHIPS):
            plane_copy(layer, group, step).wait_recv()
        sibling_copy(layer, group).start()

    def attend(layer, group):
        low, high = GROUPS[group]
        count = high - low
        keys = CORES * CHIPS * ROWS
        sibling_copy(layer, group).wait_recv()
        lane = lax.broadcasted_iota(jnp.int32, (1, keys), 1)
        slot = (lane >> 3) & 1
        biases = []
        for place in range(low, high):
            if place == 0:
                position = slot * 128 + (((lane >> 4) & 7) * 2 + (lane >> 7)) * TOK + (lane & 7)
                row = lax.broadcasted_iota(jnp.int32, (SPAN, keys), 0)
                biases.append(jnp.where(position <= row, 0.0, MASKED))
                continue
            distance = 0 if place < FIRST_FAR else DISTANCE[place - FIRST_FAR]
            holder = lax.rem(pool + POOL - distance, POOL)
            live = counts[0, pool]
            named = jnp.int32(0)
            for j in range(LIST):
                hit = ((ids[pool, layer, j] >> 6) == holder) & (j < live)
                named += jnp.where(hit, 1, 0)
            biases.append(jnp.where(slot < named, 0.0, MASKED))

        def one_head(head, carry):
            columns = pl.ds(pl.multiple_of(head * HD, HD), HD)
            rows = q[layer, :, columns]
            scores = []
            for index in range(count):
                block = lax.dot_general(
                    rows,
                    kv[layer, low + index, :, :HD],
                    (((1,), (1,)), ((), ())),
                    preferred_element_type=jnp.float32,
                )
                scores.append(block * TO_LOG2 + biases[index])
            highest = jnp.max(functools.reduce(jnp.maximum, scores), axis=1, keepdims=True)
            if group > 0:
                before = top[head]
                highest = jnp.maximum(highest, before[:, :1])
            weights = [jnp.exp2(block - highest) for block in scores]
            added = jnp.sum(functools.reduce(jnp.add, weights), axis=1, keepdims=True)
            mixed = None
            for index in range(count):
                part = jnp.dot(
                    weights[index].astype(jnp.bfloat16),
                    kv[layer, low + index, :, HD:],
                    preferred_element_type=jnp.float32,
                )
                mixed = part if mixed is None else mixed + part
            if group > 0:
                shrink = jnp.exp2(before[:, :1] - highest)
                added = added + shrink * total[head][:, :1]
                mixed = mixed + shrink * acc[head]
            if group < N_GROUPS - 1:
                top[head] = jnp.broadcast_to(highest, (SPAN, HD))
                total[head] = jnp.broadcast_to(added, (SPAN, HD))
                acc[head] = mixed
            else:
                attn[layer, :, columns] = (mixed / added).astype(jnp.bfloat16)
            return carry

        lax.fori_loop(0, QH, one_head, 0)

    def attn_copy(layer):
        return pltpu.make_async_copy(attn.at[layer], attn_out.at[layer], out_sem.at[layer])

    loads[0].wait()
    loads[1].wait()
    prepare(0)
    pl.semaphore_wait(barrier, len(DISTANCE) + CHIPS)
    z_send(0)

    @pl.loop(1, LAYERS)
    def _(layer):
        prepare(layer)
        z_send(layer)

    for place in range(POOL):
        distance = 0 if place == 0 else DISTANCE[place - 1]
        holder = pool_peer(distance)
        entry = jnp.int32(0)
        for e in range(ENTRIES):
            entry = jnp.where((new_ids[pool, e // 2, e % 2] >> 3) == holder, e, entry)
        if place == 0:
            nrecv[0] = new[entry]
        else:
            nsend[place - 1] = new[entry]
            n_copy(place - 1).start()
    origin = [jnp.int32(0)] * ENTRIES
    for place in range(POOL):
        distance = 0 if place == 0 else DISTANCE[place - 1]
        prompt = lax.rem(pool + POOL - distance, POOL)
        slot = jnp.int32(0)
        for e in range(ENTRIES):
            written = new_ids[prompt, e // 2, e % 2]
            slot = jnp.where((written >> 3) == pool, written & 7, slot)
        origin = [jnp.where(slot == j, place, origin[j]) for j in range(ENTRIES)]

    spread(0, 0)
    spread(0, 1)
    share(0, 0)
    loads[2].wait()

    @pl.loop(0, LAYERS)
    def _(layer):
        for group in range(N_GROUPS):
            if group + 2 < N_GROUPS:
                spread(layer, group + 2)
            else:

                @pl.when(layer < LAYERS - 1)
                def _():
                    spread(layer + 1, group + 2 - N_GROUPS)

            if group + 1 < N_GROUPS:
                share(layer, group + 1)
            else:

                @pl.when(layer < LAYERS - 1)
                def _():
                    share(layer + 1, 0)

            attend(layer, group)
        attn_copy(layer).start()

    for index in range(len(DISTANCE)):
        n_copy(index).wait_recv()
    for j in range(ENTRIES):
        placed[j] = nrecv[origin[j]]
    stored_copy = pltpu.make_async_copy(placed, stored_out, out_sem.at[LAYERS])
    stored_copy.start()

    @pl.loop(0, LAYERS)
    def _(layer):
        for index in range(len(DISTANCE)):
            z_copy(layer, index).wait_send()
        for group in range(N_GROUPS):
            for step in range(1, CHIPS):
                plane_copy(layer, group, step).wait_send()
            sibling_copy(layer, group).wait_send()
        attn_copy(layer).wait()

    for index in range(len(DISTANCE)):
        n_copy(index).wait_send()
    stored_copy.wait()


def body(queries, pool_cache, new_kv, block_ids, prefix_count, new_ids):
    smem = pl.BlockSpec(memory_space=pltpu.SMEM)
    hbm = pl.BlockSpec(memory_space=pl.ANY)
    bf16 = jnp.bfloat16
    far = len(DISTANCE)
    attn, stored = pl.pallas_call(
        kernel,
        out_shape=(
            jax.ShapeDtypeStruct((LAYERS, SPAN, QH * HD), bf16),
            jax.ShapeDtypeStruct((ENTRIES, HEADS * TOK, 2 * HD), bf16),
        ),
        in_specs=[smem, smem, smem, hbm, hbm, hbm],
        out_specs=(hbm, hbm),
        scratch_shapes=[
            pltpu.VMEM((SLOTS, HEADS * TOK, 2 * HD), bf16),
            pltpu.VMEM((ENTRIES, HEADS * TOK, 2 * HD), bf16),
            pltpu.VMEM((LAYERS, SPAN, QH * HD), bf16),
            pltpu.VMEM((LAYERS, far, HEADS * ROWS, 2 * HD), bf16),
            pltpu.VMEM((LAYERS, SOURCES, HEADS * ROWS, 2 * HD), bf16),
            pltpu.VMEM((LAYERS, SOURCES, CORES * CHIPS * ROWS, 2 * HD), bf16),
            pltpu.VMEM((far, HEADS * TOK, 2 * HD), bf16),
            pltpu.VMEM((POOL, HEADS * TOK, 2 * HD), bf16),
            pltpu.VMEM((ENTRIES, HEADS * TOK, 2 * HD), bf16),
            pltpu.VMEM((LAYERS, SPAN, QH * HD), bf16),
            pltpu.VMEM((QH, SPAN, HD), jnp.float32),
            pltpu.VMEM((QH, SPAN, HD), jnp.float32),
            pltpu.VMEM((QH, SPAN, HD), jnp.float32),
            pltpu.SemaphoreType.DMA((3,)),
            pltpu.SemaphoreType.DMA((LAYERS, far)),
            pltpu.SemaphoreType.DMA((LAYERS, far)),
            pltpu.SemaphoreType.DMA((LAYERS, N_GROUPS, CHIPS - 1)),
            pltpu.SemaphoreType.DMA((LAYERS, N_GROUPS, CHIPS - 1)),
            pltpu.SemaphoreType.DMA((LAYERS, N_GROUPS)),
            pltpu.SemaphoreType.DMA((LAYERS, N_GROUPS)),
            pltpu.SemaphoreType.DMA((far,)),
            pltpu.SemaphoreType.DMA((far,)),
            pltpu.SemaphoreType.DMA((LAYERS + 1,)),
        ],
        compiler_params=pltpu.CompilerParams(
            collective_id=0, has_side_effects=True, vmem_limit_bytes=48 << 20
        ),
    )(
        block_ids[0],
        prefix_count,
        new_ids[0],
        queries[0, 0],
        pool_cache.reshape(SLOTS, HEADS * TOK, 2 * HD),
        new_kv.reshape(ENTRIES, HEADS * TOK, 2 * HD),
    )
    return attn[None, None], stored.reshape(1, ENTRIES, HEADS, TOK, 2 * HD)


def solution(mesh):
    in_specs = (
        P("rep", "pool", None, None, "tp"),
        P("pool", None, "tp", None),
        P("rep", "pool", None, None, None, "tp", None),
        P("rep", None, None, None),
        P("rep", None),
        P("rep", None, None, None),
    )
    out_specs = (P("rep", "pool", None, None, "tp"), P("rep", "pool", None, "tp", None))
    return jax.shard_map(body, mesh=mesh, in_specs=in_specs, out_specs=out_specs, check_vma=False)
```

profile of v0, /device:TPU:1, one launch (start us, length us, event | category | flops | bytes accessed | tf_op | source)
XLA Modules:
  0.0 123.0 jit_solution(8257856197197765868)
XLA Ops:
  0.6 0.8 copy.9.new_ids
  1.4 0.0 copy-start
  1.4 1.6 %copy-done = bf16[1,1,4,256,1024]{4,3,2,1,0:T(8,128)(2,1)S(1)} copy-done((bf16[1,1,4,256,1024]{4,3,2,1,0:T(8,128)(2,1)S(1)}, bf16[1,1,4,256,1024]{4,3,2,1,0:T(8,128)(2,1)}, u32[]{:S(2)}) %copy-start) | copy-done | bytes 2097176
  3.0 0.0 copy-start.1
  3.0 0.9 copy-done.1
  4.0 0.0 copy-start.2
  4.0 0.7 copy-done.2
  4.7 0.0 copy-start.3
  4.7 0.7 copy-done.3
  5.3 115.7 %shard_map.77 = (bf16[4,256,1024]{2,1,0:T(8,128)(2,1)S(1)}, bf16[8,64,256]{2,1,0:T(8,128)(2,1)S(1)}) custom-call(s32[8,4,12]{2,1,0:T(4,128)S(1)} %bitcast.11, s32[1,8]{1,0:T(1,128)S(1)} %copy-done.3, s32[8,4,2]{2,1,0:T(4,128)S(1)} %copy.9.new_ids, bf16[4,256,1024]{2,1,0:T(8,128)(2,1)S(1)} %bitcast.7, bf16[64,64,256]{2,1,0:T(8,128)(2,1)} %bitcast.12, ...), custom_call_target="tpu_custom_call" | custom-call | tf_op jit(solution)/shard_map/pallas_call | solution.py:327
  121.0 1.3 %copy.14 = bf16[1,1,4,256,1024]{4,3,2,1,0:T(8,128)(2,1)} copy(bf16[1,1,4,256,1024]{4,3,2,1,0:T(8,128)(2,1)S(1)} %bitcast.8) | data formatting | bytes 4194304
  122.3 0.7 copy.15
Async XLA Ops:
  1.4 1.6 %copy-start = (bf16[1,1,4,256,1024]{4,3,2,1,0:T(8,128)(2,1)S(1)}, bf16[1,1,4,256,1024]{4,3,2,1,0:T(8,128)(2,1)}, u32[]{:S(2)}) copy-start(bf16[1,1,4,256,1024]{4,3,2,1,0:T(8,128)(2,1)} %param.6) | copy-start | bytes 6291460
  3.0 0.9 copy-start.1
  4.0 0.7 copy-start.2
  4.7 0.7 copy-start.3
where the time goes:
time: 125 us; the launch traced here: 123 us
  Pallas kernels  116 us (93%)
  local copies, waits for them, and re-layouts  6.72 us (5%)
    pallas_call x1, Pallas kernels, body(): pl.pallas_call(kernel, out_shape=(jax.ShapeDtypeStruct((LAYERS, SPAN, QH...  116 us
    unnamed x10, local copies, waits for them, and re-layouts  5.94 us

commit v1 on v0

--- a/solution.py
+++ b/solution.py
@@ -28,6 +28,7 @@
 SOURCES = FIRST_FAR + len(DISTANCE)
 GROUPS = ((0, 2), (2, 3), (3, 5), (5, 7), (7, 9))
 N_GROUPS = len(GROUPS)
+KEYS = CORES * CHIPS * ROWS
 MASKED = -1e30
 TO_LOG2 = math.log2(math.e) / math.sqrt(HD)
 
@@ -43,8 +44,9 @@
 
 
 def kernel(
-    ids, counts, new_ids, q_in, cache_in, new_in, attn_out, stored_out,
-    cache, new, q, zsend, zbuf, kv, nsend, nrecv, placed, attn, top, total, acc,
+    ids_in, counts_in, new_ids_in, q_in, cache_in, new_in, attn_out, stored_out,
+    ids, counts, new_ids,
+    cache, new, q, zsend, zbuf, kv, nsend, nrecv, placed, attn, top, total, acc, qt, flipped, causal,
     in_sem, zs, zr, ps, pr, ss, sr, ns, nr, out_sem,
 ):
     pool = lax.axis_index("pool")
@@ -60,11 +62,8 @@
 
     sibling = {"tp": chip * CORES + 1 - core}
 
-    loads = [
-        pltpu.make_async_copy(cache_in, cache, in_sem.at[0]),
-        pltpu.make_async_copy(new_in, new, in_sem.at[1]),
-        pltpu.make_async_copy(q_in, q, in_sem.at[2]),
-    ]
+    moves = ((ids_in, ids), (counts_in, counts), (new_ids_in, new_ids), (cache_in, cache), (new_in, new), (q_in, q))
+    loads = [pltpu.make_async_copy(*move, in_sem.at[index]) for index, move in enumerate(moves)]
     for load in loads:
         load.start()
 
@@ -102,7 +101,7 @@
         return pltpu.make_async_remote_copy(
             src_ref=zsend.at[layer, index],
             dst_ref=zbuf.at[layer, FIRST_FAR + index],
-            send_sem=zs.at[layer, index],
+            send_sem=zs.at[layer],
             recv_sem=zr.at[layer, index],
             device_id={"pool": pool_peer(DISTANCE[index])},
             device_id_type=MESH,
@@ -112,9 +111,19 @@
         return pltpu.make_async_remote_copy(
             src_ref=nsend.at[index],
             dst_ref=nrecv.at[1 + index],
-            send_sem=ns.at[index],
-            recv_sem=nr.at[index],
+            send_sem=ns.at[0],
+            recv_sem=nr.at[0],
             device_id={"pool": pool_peer(DISTANCE[index])},
+            device_id_type=MESH,
+        )
+
+    def whole(part, send_sem, recv_sem):
+        return pltpu.make_async_remote_copy(
+            src_ref=part,
+            dst_ref=part,
+            send_sem=send_sem,
+            recv_sem=recv_sem,
+            device_id=sibling,
             device_id_type=MESH,
         )
 
@@ -128,11 +137,16 @@
                 pl.ds(low, high - low),
                 pl.ds(pl.multiple_of((core * CHIPS + chip) * ROWS, ROWS), ROWS),
             ],
-            send_sem=ps.at[layer, group, step - 1],
-            recv_sem=pr.at[layer, group, step - 1],
+            send_sem=ps.at[layer, group],
+            recv_sem=pr.at[layer, group],
             device_id={"tp": target * CORES + core},
             device_id_type=MESH,
         )
+
+    def plane_copies(layer, group):
+        low, high = GROUPS[group]
+        part = zbuf.at[layer, pl.ds(low, high - low), pl.ds(0, (CHIPS - 1) * ROWS)]
+        return whole(part, ps.at[layer, group], pr.at[layer, group])
 
     def sibling_copy(layer, group):
         low, high = GROUPS[group]
@@ -168,23 +182,17 @@
         ] = mine
 
     def share(layer, group):
-        for step in range(1, CHIPS):
-            plane_copy(layer, group, step).wait_recv()
+        plane_copies(layer, group).wait_recv()
         sibling_copy(layer, group).start()
 
     def attend(layer, group):
         low, high = GROUPS[group]
         count = high - low
-        keys = CORES * CHIPS * ROWS
         sibling_copy(layer, group).wait_recv()
-        lane = lax.broadcasted_iota(jnp.int32, (1, keys), 1)
-        slot = (lane >> 3) & 1
         biases = []
         for place in range(low, high):
             if place == 0:
-                position = slot * 128 + (((lane >> 4) & 7) * 2 + (lane >> 7)) * TOK + (lane & 7)
-                row = lax.broadcasted_iota(jnp.int32, (SPAN, keys), 0)
-                biases.append(jnp.where(position <= row, 0.0, MASKED))
+                biases.append(None)
                 continue
             distance = 0 if place < FIRST_FAR else DISTANCE[place - FIRST_FAR]
             holder = lax.rem(pool + POOL - distance, POOL)
@@ -193,53 +201,76 @@
             for j in range(LIST):
                 hit = ((ids[pool, layer, j] >> 6) == holder) & (j < live)
                 named += jnp.where(hit, 1, 0)
-            biases.append(jnp.where(slot < named, 0.0, MASKED))
-
-        def one_head(head, carry):
-            columns = pl.ds(pl.multiple_of(head * HD, HD), HD)
-            rows = q[layer, :, columns]
+            biases.append([jnp.where(slot < named, 0.0, MASKED) for slot in range(CAP)])
+        for index in range(count):
+            values = kv[layer, low + index, :, HD:].astype(jnp.float32)
+            flipped[:, index * KEYS : (index + 1) * KEYS] = values.T.astype(jnp.bfloat16)
+
+        def score(head):
+            rows = qt[layer, head]
             scores = []
             for index in range(count):
-                block = lax.dot_general(
-                    rows,
-                    kv[layer, low + index, :, :HD],
-                    (((1,), (1,)), ((), ())),
-                    preferred_element_type=jnp.float32,
+                block = jnp.dot(
+                    kv[layer, low + index, :, :HD], rows, preferred_element_type=jnp.float32
                 )
-                scores.append(block * TO_LOG2 + biases[index])
-            highest = jnp.max(functools.reduce(jnp.maximum, scores), axis=1, keepdims=True)
+                if biases[index] is None:
+                    block = block + causal[...]
+                scores.append(block.reshape(KEYS // ROWS, CAP, TOK, SPAN))
+            return scores
+
+        def weigh(head, scores):
+            highest = None
+            for block, bias in zip(scores, biases):
+                peak = jnp.max(block, axis=0)
+                if bias is None:
+                    peak = jnp.maximum(peak[0], peak[1])
+                else:
+                    peak = jnp.maximum(peak[0] + bias[0], peak[1] + bias[1])
+                highest = peak if highest is None else jnp.maximum(highest, peak)
+            highest = jnp.max(highest, axis=0, keepdims=True) * TO_LOG2
+            shrink = None
             if group > 0:
                 before = top[head]
-                highest = jnp.maximum(highest, before[:, :1])
-            weights = [jnp.exp2(block - highest) for block in scores]
-            added = jnp.sum(functools.reduce(jnp.add, weights), axis=1, keepdims=True)
-            mixed = None
-            for index in range(count):
-                part = jnp.dot(
-                    weights[index].astype(jnp.bfloat16),
-                    kv[layer, low + index, :, HD:],
-                    preferred_element_type=jnp.float32,
-                )
-                mixed = part if mixed is None else mixed + part
+                highest = jnp.maximum(highest, before)
+                shrink = jnp.exp2(before - highest)
+            weights = []
+            added = None
+            for block, bias in zip(scores, biases):
+                shifts = [highest] * CAP if bias is None else [highest - x for x in bias]
+                shift = jnp.stack([jnp.broadcast_to(x, (TOK, SPAN)) for x in shifts])
+                weight = jnp.exp2(block * TO_LOG2 - shift[None])
+                part = jnp.sum(weight, axis=(0, 1))
+                added = part if added is None else added + part
+                weights.append(weight.reshape(KEYS, SPAN).astype(jnp.bfloat16))
+            weights = jnp.concatenate(weights, axis=0) if count > 1 else weights[0]
+            added = jnp.sum(added, axis=0, keepdims=True)
             if group > 0:
-                shrink = jnp.exp2(before[:, :1] - highest)
-                added = added + shrink * total[head][:, :1]
+                added = added + shrink * total[head]
+            total[head] = added
+            top[head] = highest
+            return weights, shrink
+
+        def mix(head, weights, shrink):
+            mixed = jnp.dot(
+                flipped[:, : count * KEYS], weights, preferred_element_type=jnp.float32
+            )
+            if group > 0:
                 mixed = mixed + shrink * acc[head]
             if group < N_GROUPS - 1:
-                top[head] = jnp.broadcast_to(highest, (SPAN, HD))
-                total[head] = jnp.broadcast_to(added, (SPAN, HD))
                 acc[head] = mixed
             else:
-                attn[layer, :, columns] = (mixed / added).astype(jnp.bfloat16)
-            return carry
-
-        lax.fori_loop(0, QH, one_head, 0)
+                attn[layer, :, head * HD : (head + 1) * HD] = (mixed / total[head]).T.astype(jnp.bfloat16)
+
+        scores = [score(head) for head in range(QH)]
+        weights = [weigh(head, scores[head]) for head in range(QH)]
+        for head in range(QH):
+            mix(head, *weights[head])
 
     def attn_copy(layer):
         return pltpu.make_async_copy(attn.at[layer], attn_out.at[layer], out_sem.at[layer])
 
-    loads[0].wait()
-    loads[1].wait()
+    for load in loads[:5]:
+        load.wait()
     prepare(0)
     pl.semaphore_wait(barrier, len(DISTANCE) + CHIPS)
     z_send(0)
@@ -254,7 +285,7 @@
         holder = pool_peer(distance)
         entry = jnp.int32(0)
         for e in range(ENTRIES):
-            entry = jnp.where((new_ids[pool, e // 2, e % 2] >> 3) == holder, e, entry)
+            entry = jnp.where((new_ids[e // 2, e % 2, pool] >> 3) == holder, e, entry)
         if place == 0:
             nrecv[0] = new[entry]
         else:
@@ -266,14 +297,27 @@
         prompt = lax.rem(pool + POOL - distance, POOL)
         slot = jnp.int32(0)
         for e in range(ENTRIES):
-            written = new_ids[prompt, e // 2, e % 2]
+            written = new_ids[e // 2, e % 2, prompt]
             slot = jnp.where((written >> 3) == pool, written & 7, slot)
         origin = [jnp.where(slot == j, place, origin[j]) for j in range(ENTRIES)]
 
     spread(0, 0)
+
+    row = lax.broadcasted_iota(jnp.int32, (KEYS, SPAN), 0)
+    position = ((row >> 3) & 1) * 128 + (((row >> 4) & 7) * 2 + (row >> 7)) * TOK + (row & 7)
+    query = lax.broadcasted_iota(jnp.int32, (KEYS, SPAN), 1)
+    causal[...] = jnp.where(position <= query, 0.0, MASKED)
+    loads[5].wait()
+
+    @pl.loop(0, LAYERS)
+    def _(layer):
+        @pl.loop(0, QH)
+        def _(head):
+            columns = pl.ds(pl.multiple_of(head * HD, HD), HD)
+            qt[layer, head] = q[layer, :, columns].astype(jnp.float32).T.astype(jnp.bfloat16)
+
     spread(0, 1)
     share(0, 0)
-    loads[2].wait()
 
     @pl.loop(0, LAYERS)
     def _(layer):
@@ -297,8 +341,7 @@
             attend(layer, group)
         attn_copy(layer).start()
 
-    for index in range(len(DISTANCE)):
-        n_copy(index).wait_recv()
+    whole(nsend, ns.at[0], nr.at[0]).wait_recv()
     for j in range(ENTRIES):
         placed[j] = nrecv[origin[j]]
     stored_copy = pltpu.make_async_copy(placed, stored_out, out_sem.at[LAYERS])
@@ -306,22 +349,19 @@
 
     @pl.loop(0, LAYERS)
     def _(layer):
-        for index in range(len(DISTANCE)):
-            z_copy(layer, index).wait_send()
+        whole(zsend.at[layer], zs.at[layer], zr.at[layer, 0]).wait_send()
         for group in range(N_GROUPS):
-            for step in range(1, CHIPS):
-                plane_copy(layer, group, step).wait_send()
+            plane_copies(layer, group).wait_send()
             sibling_copy(layer, group).wait_send()
         attn_copy(layer).wait()
 
-    for index in range(len(DISTANCE)):
-        n_copy(index).wait_send()
+    whole(nsend, ns.at[0], nr.at[0]).wait_send()
     stored_copy.wait()
 
 
 def body(queries, pool_cache, new_kv, block_ids, prefix_count, new_ids):
-    smem = pl.BlockSpec(memory_space=pltpu.SMEM)
-    hbm = pl.BlockSpec(memory_space=pl.ANY)
+    hbm = pl.BlockSpec(memory_space=pltpu.HBM)
+    anywhere = pl.BlockSpec(memory_space=pl.ANY)
     bf16 = jnp.bfloat16
     far = len(DISTANCE)
     attn, stored = pl.pallas_call(
@@ -330,9 +370,12 @@
             jax.ShapeDtypeStruct((LAYERS, SPAN, QH * HD), bf16),
             jax.ShapeDtypeStruct((ENTRIES, HEADS * TOK, 2 * HD), bf16),
         ),
-        in_specs=[smem, smem, smem, hbm, hbm, hbm],
-        out_specs=(hbm, hbm),
+        in_specs=[hbm] * 6,
+        out_specs=(anywhere, anywhere),
         scratch_shapes=[
+            pltpu.SMEM((POOL, LAYERS, LIST), jnp.int32),
+            pltpu.SMEM((1, POOL), jnp.int32),
+            pltpu.SMEM((LAYERS, ENTRIES // LAYERS, POOL), jnp.int32),
             pltpu.VMEM((SLOTS, HEADS * TOK, 2 * HD), bf16),
             pltpu.VMEM((ENTRIES, HEADS * TOK, 2 * HD), bf16),
             pltpu.VMEM((LAYERS, SPAN, QH * HD), bf16),
@@ -343,27 +386,30 @@
             pltpu.VMEM((POOL, HEADS * TOK, 2 * HD), bf16),
             pltpu.VMEM((ENTRIES, HEADS * TOK, 2 * HD), bf16),
             pltpu.VMEM((LAYERS, SPAN, QH * HD), bf16),
-            pltpu.VMEM((QH, SPAN, HD), jnp.float32),
-            pltpu.VMEM((QH, SPAN, HD), jnp.float32),
-            pltpu.VMEM((QH, SPAN, HD), jnp.float32),
-            pltpu.SemaphoreType.DMA((3,)),
+            pltpu.VMEM((QH, 1, SPAN), jnp.float32),
+            pltpu.VMEM((QH, 1, SPAN), jnp.float32),
+            pltpu.VMEM((QH, HD, SPAN), jnp.float32),
+            pltpu.VMEM((LAYERS, QH, HD, SPAN), bf16),
+            pltpu.VMEM((HD, 2 * KEYS), bf16),
+            pltpu.VMEM((KEYS, SPAN), jnp.float32),
+            pltpu.SemaphoreType.DMA((6,)),
+            pltpu.SemaphoreType.DMA((LAYERS,)),
             pltpu.SemaphoreType.DMA((LAYERS, far)),
-            pltpu.SemaphoreType.DMA((LAYERS, far)),
-            pltpu.SemaphoreType.DMA((LAYERS, N_GROUPS, CHIPS - 1)),
-            pltpu.SemaphoreType.DMA((LAYERS, N_GROUPS, CHIPS - 1)),
             pltpu.SemaphoreType.DMA((LAYERS, N_GROUPS)),
             pltpu.SemaphoreType.DMA((LAYERS, N_GROUPS)),
-            pltpu.SemaphoreType.DMA((far,)),
-            pltpu.SemaphoreType.DMA((far,)),
+            pltpu.SemaphoreType.DMA((LAYERS, N_GROUPS)),
+            pltpu.SemaphoreType.DMA((LAYERS, N_GROUPS)),
+            pltpu.SemaphoreType.DMA((1,)),
+            pltpu.SemaphoreType.DMA((1,)),
             pltpu.SemaphoreType.DMA((LAYERS + 1,)),
         ],
         compiler_params=pltpu.CompilerParams(
-            collective_id=0, has_side_effects=True, vmem_limit_bytes=48 << 20
+            collective_id=0, has_side_effects=True, vmem_limit_bytes=60 << 20
         ),
     )(
         block_ids[0],
         prefix_count,
-        new_ids[0],
+        new_ids[0].transpose(1, 2, 0),
         queries[0, 0],
         pool_cache.reshape(SLOTS, HEADS * TOK, 2 * HD),
         new_kv.reshape(ENTRIES, HEADS * TOK, 2 * HD),

time: 125 us -> 85.1 us (0.68); the launches traced: 123 us -> 84.9 us
  Pallas kernels: 116 us -> 80.5 us
  local copies, waits for them, and re-layouts: 6.72 us -> 3.83 us
    pallas_call x1, Pallas kernels: 116 us -> 80.5 us  [body(): pl.pallas_call(kernel, out_shape=(jax.ShapeDtypeStruct((LAYERS, SPAN, QH...]
    unnamed x10 -> x4, local copies, waits for them, and re-layouts: 5.94 us -> 3.83 us
where the time goes in v1:
time: 85.1 us; the launch traced here: 84.9 us
  Pallas kernels  80.5 us (95%)
  local copies, waits for them, and re-layouts  3.83 us (5%)
    pallas_call x1, Pallas kernels, body(): pl.pallas_call(kernel, out_shape=(jax.ShapeDtypeStruct((LAYERS, SPAN, QH...  80.5 us
    unnamed x4, local copies, waits for them, and re-layouts  3.83 us

profile of v1, /device:TPU:1, one launch (start us, length us, event | category | flops | bytes accessed | tf_op | source)
XLA Modules:
  0.0 84.9 jit_solution(11808657040831024887)
XLA Ops:
  0.6 80.5 %shard_map.77 = (bf16[4,256,1024]{2,1,0:T(8,128)(2,1)}, bf16[8,64,256]{2,1,0:T(8,128)(2,1)}) custom-call(s32[8,4,12]{2,1,0:T(4,128)} %bitcast.14, s32[1,8]{1,0:T(1,128)} %counts_in.1, s32[4,2,8]{2,1,0:T(2,128)} %bitcast.15, bf16[4,256,1024]{2,1,0:T(8,128)(2,1)} %bitcast.9, bf16[64,64,256]{2,1,0:T(8,128)(2,1)} %bitcast.10, bf16[8,64,256]{2,1,0:T(8,128)(2,1)} %bitcast.13), custom_call_target="tpu_custom_call" | custom-call | tf_op jit(solution)/shard_map/pallas_call | solution.py:367
  81.1 0.0 copy-start
  81.1 3.1 %copy.13 = bf16[1,1,4,256,1024]{4,3,2,1,0:T(8,128)(2,1)} copy(bf16[1,1,4,256,1024]{4,3,2,1,0:T(8,128)(2,1)} %bitcast.11) | data formatting | bytes 4194304
  84.2 0.0 copy-done
  84.2 0.7 copy.14
Async XLA Ops:
  81.1 3.1 %copy-start = (bf16[8,64,256]{2,1,0:T(8,128)(2,1)S(1)}, bf16[8,64,256]{2,1,0:T(8,128)(2,1)}, u32[]{:S(2)}) copy-start(bf16[8,64,256]{2,1,0:T(8,128)(2,1)} %get-tuple-element.5) | copy-start | bytes 786436

commit v2 on v1

--- a/solution.py
+++ b/solution.py
@@ -30,6 +30,8 @@
 N_GROUPS = len(GROUPS)
 KEYS = CORES * CHIPS * ROWS
 MASKED = -1e30
+SPREAD_AHEAD = 4
+SHARE_AHEAD = 2
 TO_LOG2 = math.log2(math.e) / math.sqrt(HD)
 
 
@@ -164,10 +166,6 @@
             device_id_type=MESH,
         )
 
-    def z_send(layer):
-        for index in range(len(DISTANCE)):
-            z_copy(layer, index).start()
-
     def spread(layer, group):
         low, high = GROUPS[group]
         for place in range(max(low, FIRST_FAR), high):
@@ -230,7 +228,7 @@
             highest = jnp.max(highest, axis=0, keepdims=True) * TO_LOG2
             shrink = None
             if group > 0:
-                before = top[head]
+                before = top[layer, head]
                 highest = jnp.maximum(highest, before)
                 shrink = jnp.exp2(before - highest)
             weights = []
@@ -245,9 +243,9 @@
             weights = jnp.concatenate(weights, axis=0) if count > 1 else weights[0]
             added = jnp.sum(added, axis=0, keepdims=True)
             if group > 0:
-                added = added + shrink * total[head]
-            total[head] = added
-            top[head] = highest
+                added = added + shrink * total[layer, head]
+            total[layer, head] = added
+            top[layer, head] = highest
             return weights, shrink
 
         def mix(head, weights, shrink):
@@ -255,11 +253,11 @@
                 flipped[:, : count * KEYS], weights, preferred_element_type=jnp.float32
             )
             if group > 0:
-                mixed = mixed + shrink * acc[head]
+                mixed = mixed + shrink * acc[layer, head]
             if group < N_GROUPS - 1:
-                acc[head] = mixed
+                acc[layer, head] = mixed
             else:
-                attn[layer, :, head * HD : (head + 1) * HD] = (mixed / total[head]).T.astype(jnp.bfloat16)
+                attn[layer, :, head * HD : (head + 1) * HD] = (mixed / total[layer, head]).T.astype(jnp.bfloat16)
 
         scores = [score(head) for head in range(QH)]
         weights = [weigh(head, scores[head]) for head in range(QH)]
@@ -273,12 +271,17 @@
         load.wait()
     prepare(0)
     pl.semaphore_wait(barrier, len(DISTANCE) + CHIPS)
-    z_send(0)
+    def send(layer):
+        spread(layer, 0)
+        for index in range(len(DISTANCE)):
+            z_copy(layer, index).start()
+
+    send(0)
 
     @pl.loop(1, LAYERS)
     def _(layer):
         prepare(layer)
-        z_send(layer)
+        send(layer)
 
     for place in range(POOL):
         distance = 0 if place == 0 else DISTANCE[place - 1]
@@ -290,7 +293,6 @@
             nrecv[0] = new[entry]
         else:
             nsend[place - 1] = new[entry]
-            n_copy(place - 1).start()
     origin = [jnp.int32(0)] * ENTRIES
     for place in range(POOL):
         distance = 0 if place == 0 else DISTANCE[place - 1]
@@ -301,44 +303,62 @@
             slot = jnp.where((written >> 3) == pool, written & 7, slot)
         origin = [jnp.where(slot == j, place, origin[j]) for j in range(ENTRIES)]
 
-    spread(0, 0)
-
     row = lax.broadcasted_iota(jnp.int32, (KEYS, SPAN), 0)
     position = ((row >> 3) & 1) * 128 + (((row >> 4) & 7) * 2 + (row >> 7)) * TOK + (row & 7)
     query = lax.broadcasted_iota(jnp.int32, (KEYS, SPAN), 1)
     causal[...] = jnp.where(position <= query, 0.0, MASKED)
     loads[5].wait()
 
+    def turn(layer):
+        for head in range(QH):
+            columns = slice(head * HD, (head + 1) * HD)
+            qt[layer, head] = q[layer, :, columns].astype(jnp.float32).T.astype(jnp.bfloat16)
+
     @pl.loop(0, LAYERS)
     def _(layer):
-        @pl.loop(0, QH)
-        def _(head):
-            columns = pl.ds(pl.multiple_of(head * HD, HD), HD)
-            qt[layer, head] = q[layer, :, columns].astype(jnp.float32).T.astype(jnp.bfloat16)
-
-    spread(0, 1)
-    share(0, 0)
+        turn(layer)
+        share(layer, 0)
 
     @pl.loop(0, LAYERS)
     def _(layer):
-        for group in range(N_GROUPS):
-            if group + 2 < N_GROUPS:
-                spread(layer, group + 2)
-            else:
-
-                @pl.when(layer < LAYERS - 1)
+        attend(layer, 0)
+        for step in range(SPREAD_AHEAD):
+
+            @pl.when(layer == min(1 + step // 2, LAYERS - 1))
+            def _():
+                spread(0, 1 + step)
+
+        for step in range(SHARE_AHEAD):
+
+            @pl.when(layer == min(2 + step, LAYERS - 1))
+            def _():
+                share(0, 1 + step)
+
+    def ahead(layer, group, steps, stage):
+        later, group = divmod(group - 1 + steps, N_GROUPS - 1)
+        if later == 0:
+            stage(layer, group + 1)
+        else:
+
+            @pl.when(layer + later < LAYERS)
+            def _():
+                stage(layer + later, group + 1)
+
+    last = divmod(N_GROUPS - 2 - SPREAD_AHEAD, N_GROUPS - 1)
+
+    @pl.loop(0, LAYERS)
+    def _(layer):
+        for group in range(1, N_GROUPS):
+            ahead(layer, group, SPREAD_AHEAD, spread)
+            if group - 1 == last[1]:
+
+                @pl.when(layer == LAYERS - 1 + last[0])
                 def _():
-                    spread(layer + 1, group + 2 - N_GROUPS)
-
-            if group + 1 < N_GROUPS:
-                share(layer, group + 1)
-            else:
-
-                @pl.when(layer < LAYERS - 1)
-                def _():
-                    share(layer + 1, 0)
+                    for index in range(len(DISTANCE)):
+                        n_copy(index).start()
 
             attend(layer, group)
+            ahead(layer, group, SHARE_AHEAD, share)
         attn_copy(layer).start()
 
     whole(nsend, ns.at[0], nr.at[0]).wait_recv()
@@ -386,11 +406,11 @@
             pltpu.VMEM((POOL, HEADS * TOK, 2 * HD), bf16),
             pltpu.VMEM((ENTRIES, HEADS * TOK, 2 * HD), bf16),
             pltpu.VMEM((LAYERS, SPAN, QH * HD), bf16),
-            pltpu.VMEM((QH, 1, SPAN), jnp.float32),
-            pltpu.VMEM((QH, 1, SPAN), jnp.float32),
-            pltpu.VMEM((QH, HD, SPAN), jnp.float32),
+            pltpu.VMEM((LAYERS, QH, 1, SPAN), jnp.float32),
+            pltpu.VMEM((LAYERS, QH, 1, SPAN), jnp.float32),
+            pltpu.VMEM((LAYERS, QH, HD, SPAN), jnp.float32),
             pltpu.VMEM((LAYERS, QH, HD, SPAN), bf16),
-            pltpu.VMEM((HD, 2 * KEYS), bf16),
+            pltpu.VMEM((HD, max(high - low for low, high in GROUPS) * KEYS), bf16),
             pltpu.VMEM((KEYS, SPAN), jnp.float32),
             pltpu.SemaphoreType.DMA((6,)),
             pltpu.SemaphoreType.DMA((LAYERS,)),

time: 85.1 us -> 72 us (0.85)
  Pallas kernels: 80.5 us -> 67.4 us
    pallas_call x1, Pallas kernels: 80.5 us -> 67.4 us  [body(): pl.pallas_call(kernel, out_shape=(jax.ShapeDtypeStruct((LAYERS, SPAN, QH...]
where the time goes in v2:
time: 72 us; the launch traced here: 71.8 us
  Pallas kernels  67.4 us (94%)
  local copies, waits for them, and re-layouts  3.83 us (5%)
    pallas_call x1, Pallas kernels, body(): pl.pallas_call(kernel, out_shape=(jax.ShapeDtypeStruct((LAYERS, SPAN, QH...  67.4 us
    unnamed x4, local copies, waits for them, and re-layouts  3.83 us

profile of v2, /device:TPU:1, one launch (start us, length us, event | category | flops | bytes accessed | tf_op | source)
XLA Modules:
  0.0 71.8 jit_solution(7264111116787809537)
XLA Ops:
  0.6 67.4 %shard_map.77 = (bf16[4,256,1024]{2,1,0:T(8,128)(2,1)}, bf16[8,64,256]{2,1,0:T(8,128)(2,1)}) custom-call(s32[8,4,12]{2,1,0:T(4,128)} %bitcast.14, s32[1,8]{1,0:T(1,128)} %counts_in.1, s32[4,2,8]{2,1,0:T(2,128)} %bitcast.15, bf16[4,256,1024]{2,1,0:T(8,128)(2,1)} %bitcast.9, bf16[64,64,256]{2,1,0:T(8,128)(2,1)} %bitcast.10, bf16[8,64,256]{2,1,0:T(8,128)(2,1)} %bitcast.13), custom_call_target="tpu_custom_call" | custom-call | tf_op jit(solution)/shard_map/pallas_call | solution.py:387
  68.0 0.0 copy-start
  68.0 3.1 %copy.13 = bf16[1,1,4,256,1024]{4,3,2,1,0:T(8,128)(2,1)} copy(bf16[1,1,4,256,1024]{4,3,2,1,0:T(8,128)(2,1)} %bitcast.11) | data formatting | bytes 4194304
  71.1 0.0 copy-done
  71.1 0.7 copy.14
Async XLA Ops:
  68.0 3.1 %copy-start = (bf16[8,64,256]{2,1,0:T(8,128)(2,1)S(1)}, bf16[8,64,256]{2,1,0:T(8,128)(2,1)}, u32[]{:S(2)}) copy-start(bf16[8,64,256]{2,1,0:T(8,128)(2,1)} %get-tuple-element.5) | copy-start | bytes 786436

commit v3 on v2

--- a/solution.py
+++ b/solution.py
@@ -23,10 +23,10 @@
 QH = 8
 SPAN = 256
 ENTRIES = 8
-DISTANCE = (4, 3, 5, 2, 6, 1, 7)
+DISTANCE = (3, 5, 2, 6, 1, 7, 4)
 FIRST_FAR = 2
 SOURCES = FIRST_FAR + len(DISTANCE)
-GROUPS = ((0, 2), (2, 3), (3, 5), (5, 7), (7, 9))
+GROUPS = ((0, 2), (2, 4), (4, 6), (6, 8), (8, 9))
 N_GROUPS = len(GROUPS)
 KEYS = CORES * CHIPS * ROWS
 MASKED = -1e30

time: 72 us -> 70.7 us (0.982)
  Pallas kernels: 67.4 us -> 66 us
    pallas_call x1, Pallas kernels: 67.4 us -> 66 us  [body(): pl.pallas_call(kernel, out_shape=(jax.ShapeDtypeStruct((LAYERS, SPAN, QH...]
where the time goes in v3:
time: 70.7 us; the launch traced here: 70.5 us
  Pallas kernels  66 us (93%)
  local copies, waits for them, and re-layouts  3.83 us (5%)
    pallas_call x1, Pallas kernels, body(): pl.pallas_call(kernel, out_shape=(jax.ShapeDtypeStruct((LAYERS, SPAN, QH...  66 us
    unnamed x4, local copies, waits for them, and re-layouts  3.83 us

profile of v3, /device:TPU:1, one launch (start us, length us, event | category | flops | bytes accessed | tf_op | source)
XLA Modules:
  0.0 70.5 jit_solution(15079183337247937730)
XLA Ops:
  0.6 66.0 %shard_map.77 = (bf16[4,256,1024]{2,1,0:T(8,128)(2,1)}, bf16[8,64,256]{2,1,0:T(8,128)(2,1)}) custom-call(s32[8,4,12]{2,1,0:T(4,128)} %bitcast.14, s32[1,8]{1,0:T(1,128)} %counts_in.1, s32[4,2,8]{2,1,0:T(2,128)} %bitcast.15, bf16[4,256,1024]{2,1,0:T(8,128)(2,1)} %bitcast.9, bf16[64,64,256]{2,1,0:T(8,128)(2,1)} %bitcast.10, bf16[8,64,256]{2,1,0:T(8,128)(2,1)} %bitcast.13), custom_call_target="tpu_custom_call" | custom-call | tf_op jit(solution)/shard_map/pallas_call | solution.py:387
  66.7 0.0 copy-start
  66.7 3.1 %copy.13 = bf16[1,1,4,256,1024]{4,3,2,1,0:T(8,128)(2,1)} copy(bf16[1,1,4,256,1024]{4,3,2,1,0:T(8,128)(2,1)} %bitcast.11) | data formatting | bytes 4194304
  69.8 0.0 copy-done
  69.8 0.7 copy.14
Async XLA Ops:
  66.7 3.1 %copy-start = (bf16[8,64,256]{2,1,0:T(8,128)(2,1)S(1)}, bf16[8,64,256]{2,1,0:T(8,128)(2,1)}, u32[]{:S(2)}) copy-start(bf16[8,64,256]{2,1,0:T(8,128)(2,1)} %get-tuple-element.5) | copy-start | bytes 786436

commit v4 on v3

--- a/solution.py
+++ b/solution.py
@@ -31,7 +31,7 @@
 KEYS = CORES * CHIPS * ROWS
 MASKED = -1e30
 SPREAD_AHEAD = 4
-SHARE_AHEAD = 2
+SHARE_AHEAD = 3
 TO_LOG2 = math.log2(math.e) / math.sqrt(HD)
 
 

time: 70.7 us -> 71.7 us (1.014)
  no operation moved by 1% of the time
where the time goes in v4:
time: 71.7 us; the launch traced here: 71 us
  Pallas kernels  66.5 us (93%)
  local copies, waits for them, and re-layouts  3.83 us (5%)
    pallas_call x1, Pallas kernels, body(): pl.pallas_call(kernel, out_shape=(jax.ShapeDtypeStruct((LAYERS, SPAN, QH...  66.5 us
    unnamed x4, local copies, waits for them, and re-layouts  3.83 us

profile of v4, /device:TPU:1, one launch (start us, length us, event | category | flops | bytes accessed | tf_op | source)
XLA Modules:
  0.0 71.0 jit_solution(1165501189374962980)
XLA Ops:
  0.6 66.5 %shard_map.77 = (bf16[4,256,1024]{2,1,0:T(8,128)(2,1)}, bf16[8,64,256]{2,1,0:T(8,128)(2,1)}) custom-call(s32[8,4,12]{2,1,0:T(4,128)} %bitcast.14, s32[1,8]{1,0:T(1,128)} %counts_in.1, s32[4,2,8]{2,1,0:T(2,128)} %bitcast.15, bf16[4,256,1024]{2,1,0:T(8,128)(2,1)} %bitcast.9, bf16[64,64,256]{2,1,0:T(8,128)(2,1)} %bitcast.10, bf16[8,64,256]{2,1,0:T(8,128)(2,1)} %bitcast.13), custom_call_target="tpu_custom_call" | custom-call | tf_op jit(solution)/shard_map/pallas_call | solution.py:387
  67.1 0.0 copy-start
  67.2 3.1 %copy.13 = bf16[1,1,4,256,1024]{4,3,2,1,0:T(8,128)(2,1)} copy(bf16[1,1,4,256,1024]{4,3,2,1,0:T(8,128)(2,1)} %bitcast.11) | data formatting | bytes 4194304
  70.3 0.0 copy-done
  70.3 0.7 copy.14
Async XLA Ops:
  67.1 3.1 %copy-start = (bf16[8,64,256]{2,1,0:T(8,128)(2,1)S(1)}, bf16[8,64,256]{2,1,0:T(8,128)(2,1)}, u32[]{:S(2)}) copy-start(bf16[8,64,256]{2,1,0:T(8,128)(2,1)} %get-tuple-element.5) | copy-start | bytes 786436
